TPU v7x, 512 devices: a whole 4x4x16 slice. The times are simulated.
512 devices in a mesh: tile: 32 (over x, z_hi, core), dir: 16 (over y, z_lo).
Axes of the slice: x: 4, y: 4, z: 16 (z_hi: 4, z_lo: 4; z = z_hi * 4 + z_lo), core: 2. Of those that a mesh axis runs over, the one named last changes fastest.
Arguments:
- background_prev: float32 [64, 256, 128], P(None, 'tile'), may hold values from -6 to 6
- background_now: float32 [64, 256, 128], P(None, 'tile'), may hold values from -6 to 6
- stiffness: bfloat16 [64, 256, 128], P(None, 'tile'), may hold values from 0.039794922 to 0.19921875
- drift_terms: bfloat16 [3, 64, 256, 128], P(None, None, 'tile'), may hold values from -0.079589844 to 0.079589844
- born_prev: bfloat16 [64, 64, 256, 128], P('dir', None, 'tile'), may hold values from -6 to 6
- born_now: bfloat16 [64, 64, 256, 128], P('dir', None, 'tile'), may hold values from -6 to 6
- pieces: bfloat16 [64, 1024, 32, 128], P('dir', 'tile'), may hold values from -6 to 6
- piece_target: int32 [1024, 1], P('tile'), may hold values from 0 to 31; in each aligned block of 32 rows (0 to 31, 32 to 63, ...) at most 2 rows name the same one
- piece_block: int32 [1024], P('tile'), may hold values from 0 to 15
- wavelet: float32 [4], replicated, may hold values from -24 to 24
- source_cell: int32 [3], replicated, may hold values from 0 to 63
- receiver_z: int32 [256], replicated, may hold values from 0 to 63
- receiver_x: int32 [256], replicated, may hold values from 0 to 255
- receiver_y: int32 [256], replicated, may hold values from 0 to 127
Outputs:
- born_field: float32 [64, 64, 256, 128], P('dir', None, 'tile')
- traces: float32 [64, 4, 256], P('dir')
Inputs may be any that keep to these rules, and one draw needn't show every extreme that they name: `piece_target`: in each aligned block of 32 rows (the rows of one device) no tile is named by more than 2 rows; in some blocks a tile is named by exactly 2 rows.
All inputs are finite; a program needn't handle non-finite values.
Results may differ from a plain program's by a relative error of at most 0.0005.
Values may be sent and summed in bfloat16 or wider, within the bound.
No kernel may reach another device: no remote copies, remote signals or barrier semaphores. Data moves between devices by JAX's collectives and lax.ppermute only.
A program may use at most 128 MiB of HBM per device.

v0:
```python
import jax
import jax.numpy as jnp
from jax import lax
from jax.sharding import PartitionSpec as P

CX = 8
ITERS = 4
ZPARTS = 2
CAP = 2
SECOND_TAPS = (-205.0 / 72.0, 8.0 / 5.0, -1.0 / 5.0, 8.0 / 315.0, -1.0 / 560.0)
FIRST_TAPS = (0.0, 4.0 / 5.0, -1.0 / 5.0, 4.0 / 105.0, -1.0 / 280.0)


def padded_2(block, sides, width):
    for axis, dim in sides:
        count = lax.axis_size(axis)
        forward = [(i, i + 1) for i in range(count - 1)]
        backward = [(target, source) for source, target in forward]
        low = lax.ppermute(
            lax.slice_in_dim(block, block.shape[dim] - width, None, axis=dim), axis, forward
        )
        high = lax.ppermute(lax.slice_in_dim(block, 0, width, axis=dim), axis, backward)
        block = jnp.concatenate([low, block, high], axis=dim)
    return block


def shifted(padded, interior, spatial, offset):
    starts = [4, 4, 4]
    starts[spatial] = 4 + offset
    leading = padded.ndim - 3
    window = tuple(
        [slice(None)] * leading
        + [slice(starts[which], starts[which] + interior[which]) for which in range(3)]
    )
    return padded[window]


def operate(padded, stiff_wide, drift_wide):
    interior = stiff_wide.shape
    center = shifted(padded, interior, 0, 0)
    second = 3.0 * SECOND_TAPS[0] * center
    slopes = jnp.zeros_like(center)
    for spatial in range(3):
        gradient = jnp.zeros_like(center)
        for offset in range(1, 5):
            forward = shifted(padded, interior, spatial, offset)
            backward = shifted(padded, interior, spatial, -offset)
            second = second + SECOND_TAPS[offset] * (forward + backward)
            gradient = gradient + FIRST_TAPS[offset] * (forward - backward)
        slopes = slopes + drift_wide[spatial] * gradient
    return stiff_wide * second + slopes


def faces(born_present, background_part):
    return (padded_2(born_present, (("tile", 2),), 4), padded_2(background_part, (("tile", 2),), 4))


def assemble(pieces, piece_target, piece_block, tile_count):
    targets = piece_target[:, 0]
    row_count = targets.shape[0]
    positions = jnp.arange(row_count)
    before = (targets[:, None] == targets[None, :]) & (positions[None, :] < positions[:, None])
    arrival = jnp.sum(before.astype(jnp.int32), axis=1)
    slot_ids = targets * CAP + arrival
    placing = (slot_ids[:, None] == jnp.arange(tile_count * CAP)[None, :]).astype(jnp.bfloat16)
    outgoing = jnp.einsum(
        "krzy,rs->kszy", pieces, placing, preferred_element_type=jnp.float32
    ).astype(jnp.bfloat16)
    labels = jnp.dot(
        (piece_block + 1).astype(jnp.bfloat16)[None, :], placing, preferred_element_type=jnp.float32
    ).astype(jnp.bfloat16)
    incoming, arrived = (
        lax.all_to_all(outgoing, "tile", split_axis=1, concat_axis=1, tiled=True),
        lax.all_to_all(labels, "tile", split_axis=1, concat_axis=1, tiled=True),
    )
    wanted = (jnp.arange(ZPARTS * CX) + 1).astype(jnp.float32)
    picking = (
        (arrived[0][:, None].astype(jnp.float32) == wanted[None, :])
        .astype(jnp.bfloat16)
        .reshape(-1, ZPARTS, CX)
    )
    perturb = jnp.einsum("kszy,spx->kpzxy", incoming, picking, preferred_element_type=jnp.float32)
    return perturb.reshape(pieces.shape[0], ZPARTS * pieces.shape[2], CX, pieces.shape[3])


def local(
    background_prev,
    background_now,
    stiffness,
    drift_terms,
    born_prev,
    born_now,
    pieces,
    piece_target,
    piece_block,
    wavelet,
    source_cell,
    receiver_z,
    receiver_x,
    receiver_y,
):
    tile_count = lax.axis_size("tile")
    tile_place = lax.axis_index("tile")
    depth_cells, width_cells, height_cells = background_now.shape
    stiff_wide = stiffness.astype(jnp.float32)
    drift_wide = drift_terms.astype(jnp.float32)
    perturb = assemble(pieces, piece_target, piece_block, tile_count)
    across_axis = (tile_place * width_cells + jnp.arange(width_cells))[None, :, None]
    height_axis = jnp.arange(height_cells)[None, None, :]
    earlier_born = born_prev.astype(jnp.float32)
    current_born = born_now.astype(jnp.float32)
    local_x = receiver_x - tile_place * width_cells
    inside = ((local_x >= 0) & (local_x < width_cells)).astype(jnp.float32)
    flat_index = (
        receiver_z * width_cells + jnp.clip(local_x, 0, width_cells - 1)
    ) * height_cells + receiver_y
    slab_cells = depth_cells // lax.axis_size("dir")
    slab_start = lax.axis_index("dir") * slab_cells
    previous = lax.dynamic_slice_in_dim(background_prev, slab_start, slab_cells, 0)
    present = lax.dynamic_slice_in_dim(background_now, slab_start, slab_cells, 0)
    slab_stiff = lax.dynamic_slice_in_dim(stiff_wide, slab_start, slab_cells, 0)
    slab_drift = lax.dynamic_slice_in_dim(drift_wide, slab_start, slab_cells, 1)
    depth_axis = (slab_start + jnp.arange(slab_cells))[:, None, None]
    source_mask = (
        (depth_axis == source_cell[0])
        & (across_axis == source_cell[1])
        & (height_axis == source_cell[2])
    ).astype(jnp.float32)
    records = []
    for step_index in range(ITERS):
        deeper = padded_2(present[None], (("dir", 1),), 4)
        born_wide, back_wide = faces(current_born, deeper)
        local_accel = operate(
            jnp.pad(back_wide[0], ((0, 0), (0, 0), (4, 4))), slab_stiff, slab_drift
        )
        acceleration = lax.all_gather(local_accel, "dir", axis=0, tiled=True)
        previous, present = (
            present,
            2.0 * present - previous + local_accel + wavelet[step_index] * source_mask,
        )
        born_padded = jnp.pad(born_wide, ((0, 0), (4, 4), (0, 0), (4, 4)))
        following = (
            2.0 * current_born
            - earlier_born
            + operate(born_padded, stiff_wide, drift_wide)
            + perturb * acceleration
        )
        records.append(
            jnp.take(following.reshape(following.shape[0], -1), flat_index, axis=1)
            * inside[None, :]
        )
        earlier_born, current_born = (current_born, following)
    traces = lax.psum(jnp.stack(records, axis=1), "tile")
    return (current_born, traces)


def solution(mesh):
    placed = (
        P(None, "tile", None),
        P(None, "tile", None),
        P(None, "tile", None),
        P(None, None, "tile", None),
        P("dir", None, "tile", None),
        P("dir", None, "tile", None),
        P("dir", "tile", None, None),
        P("tile", None),
        P("tile"),
        P(),
        P(),
        P(),
        P(),
        P(),
    )
    return jax.shard_map(
        local,
        mesh=mesh,
        in_specs=placed,
        out_specs=(P("dir", None, "tile", None), P("dir", None, None)),
        check_vma=False,
    )
```

profile of v0, /device:TPU:24, one launch (start us, length us, event | category | flops | bytes accessed | tf_op | source)
XLA Modules:
  0.0 746.2 jit_solution(9172707135732427772)
XLA Ops:
  3.8 17.9 %all-to-all-start = ((bf16[1,32,2]{2,0,1:T(2,128)(2,1)}), bf16[1,32,2]{2,0,1:T(2,128)(2,1)S(1)}, u32[]{:S(2)}, u32[]{:S(2)}) async-start(bf16[1,32,2]{2,0,1:T(2,128)(2,1)} %all_to_all.12), calls=%async_computation | async-start | bytes 32768 | tf_op jit(solution)/shard_map/all_to_all | solution.py:74
  22.6 2.8 copy.42
  25.4 10.8 %all-to-all-done = bf16[1,32,2]{2,0,1:T(2,128)(2,1)S(1)} async-done(((bf16[1,32,2]{2,0,1:T(2,128)(2,1)}), bf16[1,32,2]{2,0,1:T(2,128)(2,1)S(1)}, u32[]{:S(2)}, u32[]{:S(2)}) %all-to-all-start) | async-done | bytes 160 | tf_op jit(solution)/shard_map/all_to_all | solution.py:74
  36.3 4.8 all-to-all-start.1
  41.8 4.0 collective-permute-start.3
  45.8 1.9 collective-permute-start.2
  50.1 3.8 collective-permute-start
  57.7 67.6 %collective-permute-done.3 = f32[1,4,8,128]{3,2,1,0:T(8,128)S(1)} collective-permute-done((f32[1,4,8,128]{3,2,1,0:T(8,128)S(1)}, f32[1,4,8,128]{3,2,1,0:T(8,128)S(1)}, u32[]{:S(2)}, u32[]{:S(2)}) %collective-permute-start.3) | collective-permute-done | bytes 16416 | tf_op jit(solution)/shard_map/ppermute | solution.py:22
  126.7 3.0 collective-permute-start.4
  130.6 1.5 fusion.39
  132.1 27.6 %collective-permute-start.9 = (f32[1,4,8,128]{3,2,1,0:T(8,128)S(1)}, f32[1,4,8,128]{3,2,1,0:T(8,128)S(1)}, u32[]{:S(2)}, u32[]{:S(2)}) collective-permute-start(f32[1,4,8,128]{3,2,1,0:T(8,128)S(1)} %bitcast.136), channel_id=1, source_target_pairs={{1,0},{2,1},{3,2},{4,3},{5,4},{6,5},{7,6},{8,7},{9,8},{10,9},{11,1... | collective-permute-start | bytes 49160 | tf_op jit(solution)/shard_map/ppermute | solution.py:22
  159.8 1.9 collective-permute-start.8
  161.9 6.2 collective-permute-done.8
  169.4 10.4 %collective-permute-start.10 = (f32[1,12,4,128]{3,2,1,0:T(4,128)S(1)}, f32[1,12,4,128]{3,2,1,0:T(4,128)S(1)}, u32[]{:S(2)}, u32[]{:S(2)}) collective-permute-start(f32[1,12,4,128]{3,2,1,0:T(4,128)S(1)} %get-tuple-element.30), channel_id=1, source_target_pairs={{0,16},{16,32},{32,48},{48,64},{64,80},{80,96},{96,112},{112,128},... | collective-permute-start | bytes 73736 | tf_op jit(solution)/shard_map/ppermute | solution.py:19
  179.8 37.0 %all_gather.12 = f32[64,8,128]{2,1,0:T(8,128)} all-gather(f32[4,8,128]{2,1,0:T(8,128)S(1)} %get-tuple-element.14), channel_id=1, replica_groups=mesh['tile'=32,'dir'=16] {'dir'}, dimensions={0}, use_global_device_ids=true | all-gather | bytes 278528 | tf_op jit(solution)/shard_map/all_gather | solution.py:136
  216.8 1.5 fusion.108
  218.3 3.6 collective-permute-start.15
  221.9 2.2 collective-permute-start.14
  224.2 5.3 select_maximum_fusion.6
  229.5 3.0 fusion.6
  232.5 7.7 %multiply_add_fusion.3 = f32[4,64,8,128]{3,2,1,0:T(8,128)S(1)} fusion(f32[4,64,8,128]{3,2,1,0:T(8,128)S(1)} %bitcast.132, f32[4,72,16,136]{3,2,1,0:T(8,128)S(1)} %copy-done.2, f32[4,64,4,128]{3,2,1,0:T(4,128)S(1)} %copy-done.15, f32[4,64,8,128]{3,2,1,0:T(8,128)S(1)} %convert_element_type.62, f32[4,64,4,128]{3,2,1,0:T(4,128)} %collective-permute-done, ...), kind=kLoop, calls=%fused_computation.110 | loop fusion | flops 23855104 | bytes 22806528 | tf_op jit(solution)/shard_map/add | solution.py:143
  240.4 1.4 collective-permute-start.7
  241.9 3.1 collective-permute-start.6
  246.3 7.5 collective-permute-start.16
  253.7 49.0 %all_gather.13 = f32[64,8,128]{2,1,0:T(8,128)S(1)} all-gather(f32[4,8,128]{2,1,0:T(8,128)S(1)} %get-tuple-element.12), channel_id=1, replica_groups=mesh['tile'=32,'dir'=16] {'dir'}, dimensions={0}, use_global_device_ids=true | all-gather | bytes 278528 | tf_op jit(solution)/shard_map/all_gather | solution.py:136
  302.8 2.7 select_maximum_fusion.4
  305.5 6.1 multiply_add_fusion.2
  313.1 3.1 collective-permute-start.12
  316.1 2.2 fusion.42
  318.4 3.2 collective-permute-start.21
  321.5 3.0 collective-permute-start.20
  324.5 46.2 %all_gather.14 = f32[64,8,128]{2,1,0:T(8,128)S(1)} all-gather(f32[4,8,128]{2,1,0:T(8,128)S(1)} %get-tuple-element.10), channel_id=1, replica_groups=mesh['tile'=32,'dir'=16] {'dir'}, dimensions={0}, use_global_device_ids=true | all-gather | bytes 278528 | tf_op jit(solution)/shard_map/all_gather | solution.py:136
  372.0 3.2 collective-permute-start.22
  375.2 2.7 select_maximum_fusion.2
  377.9 6.1 multiply_add_fusion.1
  387.4 11.4 %collective-permute-start.18 = (f32[4,64,4,128]{3,2,1,0:T(4,128)}, f32[4,64,4,128]{3,2,1,0:T(4,128)}, u32[]{:S(2)}, u32[]{:S(2)}) collective-permute-start(f32[4,64,4,128]{3,2,1,0:T(4,128)} %get-tuple-element.15), channel_id=1, source_target_pairs={{0,16},{16,32},{32,48},{48,64},{64,80},{80,96},{96,112},{112,128},... | collective-permute-start | bytes 1572872 | tf_op jit(solution)/shard_map/ppermute | solution.py:19
  399.7 48.9 %all_gather.15 = f32[64,8,128]{2,1,0:T(8,128)} all-gather(f32[4,8,128]{2,1,0:T(8,128)S(1)} %fusion.56), channel_id=1, replica_groups=mesh['tile'=32,'dir'=16] {'dir'}, dimensions={0}, use_global_device_ids=true | all-gather | bytes 278528 | tf_op jit(solution)/shard_map/all_gather | solution.py:136
  448.6 15.9 %copy.45 = f32[4,64,8,128]{0,3,2,1:T(8,128)} copy(f32[4,64,8,128]{3,2,1,0:T(8,128)S(1)} %multiply_add_fusion.3) | data formatting | bytes 2097152 | tf_op jit(solution)/shard_map/add | solution.py:143
  464.6 11.3 %gather_fusion = f32[256,4]{1,0:T(8,128)S(1)} fusion(f32[4,65536]{0,1:T(8,128)} %bitcast.128, s32[1024]{0:T(1024)S(1)} %pad_clamp_fusion), kind=kCustom, calls=%fused_computation.clone | custom fusion | bytes 9216 | tf_op jit(solution)/shard_map/jit(_take)/gather | solution.py:149
  475.8 16.0 %copy.46 = f32[4,64,8,128]{0,3,2,1:T(8,128)} copy(f32[4,64,8,128]{3,2,1,0:T(8,128)S(1)} %multiply_add_fusion.2) | data formatting | bytes 2097152 | tf_op jit(solution)/shard_map/add | solution.py:143
  491.8 11.9 %gather_fusion.1 = f32[256,4]{1,0:T(8,128)} fusion(f32[4,65536]{0,1:T(8,128)} %bitcast.130, s32[1024]{0:T(1024)S(1)} %pad_clamp_fusion), kind=kCustom, calls=%fused_computation.1.clone | custom fusion | bytes 9216 | tf_op jit(solution)/shard_map/jit(_take)/gather | solution.py:149
  503.7 16.0 %copy.47 = f32[4,64,8,128]{0,3,2,1:T(8,128)} copy(f32[4,64,8,128]{3,2,1,0:T(8,128)S(1)} %copy-done.4) | data formatting | bytes 2097152 | tf_op jit(solution)/shard_map/add | solution.py:143
  519.7 11.9 %gather_fusion.2 = f32[256,4]{1,0:T(8,128)} fusion(f32[4,65536]{0,1:T(8,128)} %bitcast.131, s32[1024]{0:T(1024)S(1)} %pad_clamp_fusion), kind=kCustom, calls=%fused_computation.2.clone | custom fusion | bytes 9216 | tf_op jit(solution)/shard_map/jit(_take)/gather | solution.py:149
  531.6 3.8 select_maximum_fusion
  535.4 8.5 %multiply_add_fusion = f32[4,64,8,128]{3,2,1,0:T(8,128)} fusion(f32[4,64,8,128]{3,2,1,0:T(8,128)S(1)} %bitcast.135, f32[4,72,16,136]{3,2,1,0:T(8,128)S(1)} %select_maximum_fusion, f32[4,64,4,128]{3,2,1,0:T(4,128)} %collective-permute-done.19, f32[4,64,8,128]{3,2,1,0:T(8,128)S(1)} %copy-done.4, f32[4,64,4,128]{3,2,1,0:T(4,128)} %collective-permute-done.18, ...), kind=kLoop, calls=%fused_computation.107 | loop fusion | flops 23592960 | bytes 23330816 | tf_op jit(solution)/shard_map/add | solution.py:143
  543.9 16.9 %copy.48 = f32[4,64,8,128]{0,3,2,1:T(8,128)} copy(f32[4,64,8,128]{3,2,1,0:T(8,128)} %multiply_add_fusion) | data formatting | bytes 2097152 | tf_op jit(solution)/shard_map/add | solution.py:143
  560.8 11.3 %gather_fusion.3 = f32[256,4]{1,0:T(8,128)S(1)} fusion(f32[4,65536]{0,1:T(8,128)} %bitcast.129, s32[1024]{0:T(1024)S(1)} %pad_clamp_fusion), kind=kCustom, calls=%fused_computation.3.clone | custom fusion | bytes 9216 | tf_op jit(solution)/shard_map/jit(_take)/gather | solution.py:149
  572.6 173.6 %psum.7 = f32[4,4,256]{2,1,0:T(4,128)} all-reduce(f32[4,4,256]{2,1,0:T(4,128)S(1)} %pad_maximum_fusion.12), channel_id=1, replica_groups=mesh['tile'=32,'dir'=16] {'tile'}, use_global_device_ids=true, to_apply=%region_1.3 | all-reduce | flops 4096 | bytes 32768 | tf_op jit(solution)/shard_map/psum | solution.py:153
  (127 shorter events, 23.7 us)
Async XLA Ops:
  0.6 21.2 %copy-start = (bf16[4,32,32,128]{3,2,1,0:T(8,128)(2,1)S(1)}, bf16[4,32,32,128]{3,2,1,0:T(8,128)(2,1)}, u32[]{:S(2)}) copy-start(bf16[4,32,32,128]{3,2,1,0:T(8,128)(2,1)} %param.22) | copy-start | bytes 3145732
  3.8 32.4 %all-to-all-start = ((bf16[1,32,2]{2,0,1:T(2,128)(2,1)}), bf16[1,32,2]{2,0,1:T(2,128)(2,1)S(1)}, u32[]{:S(2)}, u32[]{:S(2)}) async-start(bf16[1,32,2]{2,0,1:T(2,128)(2,1)} %all_to_all.12), calls=%async_computation | async-start | bytes 32768 | tf_op jit(solution)/shard_map/all_to_all | solution.py:74
  22.6 25.1 %copy-start.5 = (bf16[4,64,8,128]{3,2,1,0:T(8,128)(2,1)S(1)}, bf16[4,64,8,128]{3,2,1,0:T(8,128)(2,1)}, u32[]{:S(2)}) copy-start(bf16[4,64,8,128]{3,2,1,0:T(8,128)(2,1)} %param.21) | copy-start | bytes 1572868
  22.6 31.3 %copy-start.17 = (bf16[3,64,8,128]{3,2,1,0:T(8,128)(2,1)S(1)}, bf16[3,64,8,128]{3,2,1,0:T(8,128)(2,1)}, u32[]{:S(2)}) copy-start(bf16[3,64,8,128]{3,2,1,0:T(8,128)(2,1)} %param.19) | copy-start | bytes 1179652
  25.4 28.6 %copy-start.21 = (s32[3]{0:T(128)S(1)}, s32[3]{0:T(128)}, u32[]{:S(2)}) copy-start(s32[3]{0:T(128)} %param.26) | copy-start | bytes 40
  25.4 30.6 %copy-start.22 = (f32[4]{0:T(128)S(1)}, f32[4]{0:T(128)}, u32[]{:S(2)}) copy-start(f32[4]{0:T(128)} %param.25) | copy-start | bytes 52
  25.4 31.4 %copy-start.23 = (s32[256]{0:T(256)S(1)}, s32[256]{0:T(256)}, u32[]{:S(2)}) copy-start(s32[256]{0:T(256)} %param.29) | copy-start | bytes 3076
  25.4 31.4 %copy-start.24 = (s32[256]{0:T(256)S(1)}, s32[256]{0:T(256)}, u32[]{:S(2)}) copy-start(s32[256]{0:T(256)} %param.28) | copy-start | bytes 3076
  25.4 31.4 %copy-start.25 = (s32[256]{0:T(256)S(1)}, s32[256]{0:T(256)}, u32[]{:S(2)}) copy-start(s32[256]{0:T(256)} %param.27) | copy-start | bytes 3076
  25.4 105.0 %copy-start.20 = (bf16[64,8,128]{2,1,0:T(8,128)(2,1)S(1)}, bf16[64,8,128]{2,1,0:T(8,128)(2,1)}, u32[]{:S(2)}) copy-start(bf16[64,8,128]{2,1,0:T(8,128)(2,1)} %param.18) | copy-start | bytes 393220
  36.3 193.2 %all-to-all-start.1 = ((bf16[4,64,32,128]{3,2,0,1:T(8,128)(2,1)}), bf16[4,64,32,128]{3,2,0,1:T(8,128)(2,1)}, u32[]{:S(2)}, u32[]{:S(2)}) async-start(bf16[4,64,32,128]{3,2,0,1:T(8,128)(2,1)} %copy.42), calls=%async_computation.1 | async-start | bytes 4194304 | tf_op jit(solution)/shard_map/all_to_all | solution.py:73
  41.8 83.6 %collective-permute-start.3 = (f32[1,4,8,128]{3,2,1,0:T(8,128)S(1)}, f32[1,4,8,128]{3,2,1,0:T(8,128)S(1)}, u32[]{:S(2)}, u32[]{:S(2)}) collective-permute-start(f32[1,4,8,128]{3,2,1,0:T(8,128)S(1)} %dynamic-slice_bitcast_fusion.3), channel_id=1, source_target_pairs={{1,0},{2,1},{3,2},{4,3},{5,4},{6,5},{7,6},{8,7},{9,8},{10,9},{11,1... | collective-permute-start | bytes 49160 | tf_op jit(solution)/shard_map/ppermute | solution.py:22
  45.8 79.6 %collective-permute-start.2 = (f32[1,4,8,128]{3,2,1,0:T(8,128)S(1)}, f32[1,4,8,128]{3,2,1,0:T(8,128)S(1)}, u32[]{:S(2)}, u32[]{:S(2)}) collective-permute-start(f32[1,4,8,128]{3,2,1,0:T(8,128)S(1)} %dynamic-slice_bitcast_fusion.3), channel_id=1, source_target_pairs={{0,1},{1,2},{2,3},{3,4},{4,5},{5,6},{6,7},{7,8},{8,9},{9,10},{10,1... | collective-permute-start | bytes 49160 | tf_op jit(solution)/shard_map/ppermute | solution.py:19
  48.8 175.3 %collective-permute-start.1 = (f32[4,64,4,128]{3,2,1,0:T(4,128)}, f32[4,64,4,128]{3,2,1,0:T(4,128)S(1)}, u32[]{:S(2)}, u32[]{:S(2)}) collective-permute-start(f32[4,64,4,128]{3,2,1,0:T(4,128)} %get-tuple-element.25), channel_id=1, source_target_pairs={{16,0},{32,16},{48,32},{64,48},{80,64},{96,80},{112,96},{128,112},... | collective-permute-start | bytes 1572872 | tf_op jit(solution)/shard_map/ppermute | solution.py:22
  50.1 174.0 %collective-permute-start = (f32[4,64,4,128]{3,2,1,0:T(4,128)}, f32[4,64,4,128]{3,2,1,0:T(4,128)}, u32[]{:S(2)}, u32[]{:S(2)}) collective-permute-start(f32[4,64,4,128]{3,2,1,0:T(4,128)} %get-tuple-element.24), channel_id=1, source_target_pairs={{0,16},{16,32},{32,48},{48,64},{64,80},{80,96},{96,112},{112,128},... | collective-permute-start | bytes 1572872 | tf_op jit(solution)/shard_map/ppermute | solution.py:19
  54.0 175.4 %copy-start.13 = (f32[3,64,8,128]{3,2,1,0:T(8,128)}, f32[3,64,8,128]{3,2,1,0:T(8,128)S(1)}, u32[]{:S(2)}) copy-start(f32[3,64,8,128]{3,2,1,0:T(8,128)S(1)} %convert_element_type.65) | copy-start | bytes 2359300
  125.4 5.1 collective-permute-start.5
  126.7 3.9 collective-permute-start.4
  132.1 29.7 %collective-permute-start.9 = (f32[1,4,8,128]{3,2,1,0:T(8,128)S(1)}, f32[1,4,8,128]{3,2,1,0:T(8,128)S(1)}, u32[]{:S(2)}, u32[]{:S(2)}) collective-permute-start(f32[1,4,8,128]{3,2,1,0:T(8,128)S(1)} %bitcast.136), channel_id=1, source_target_pairs={{1,0},{2,1},{3,2},{4,3},{5,4},{6,5},{7,6},{8,7},{9,8},{10,9},{11,1... | collective-permute-start | bytes 49160 | tf_op jit(solution)/shard_map/ppermute | solution.py:22
  159.8 8.3 %collective-permute-start.8 = (f32[1,4,8,128]{3,2,1,0:T(8,128)S(1)}, f32[1,4,8,128]{3,2,1,0:T(8,128)S(1)}, u32[]{:S(2)}, u32[]{:S(2)}) collective-permute-start(f32[1,4,8,128]{3,2,1,0:T(8,128)S(1)} %bitcast.137), channel_id=1, source_target_pairs={{0,1},{1,2},{2,3},{3,4},{4,5},{5,6},{6,7},{7,8},{8,9},{9,10},{10,1... | collective-permute-start | bytes 49160 | tf_op jit(solution)/shard_map/ppermute | solution.py:19
  168.1 48.6 %collective-permute-start.11 = (f32[1,12,4,128]{3,2,1,0:T(4,128)S(1)}, f32[1,12,4,128]{3,2,1,0:T(4,128)S(1)}, u32[]{:S(2)}, u32[]{:S(2)}) collective-permute-start(f32[1,12,4,128]{3,2,1,0:T(4,128)S(1)} %get-tuple-element.31), channel_id=1, source_target_pairs={{16,0},{32,16},{48,32},{64,48},{80,64},{96,80},{112,96},{128,112},... | collective-permute-start | bytes 73736 | tf_op jit(solution)/shard_map/ppermute | solution.py:22
  169.4 47.3 %collective-permute-start.10 = (f32[1,12,4,128]{3,2,1,0:T(4,128)S(1)}, f32[1,12,4,128]{3,2,1,0:T(4,128)S(1)}, u32[]{:S(2)}, u32[]{:S(2)}) collective-permute-start(f32[1,12,4,128]{3,2,1,0:T(4,128)S(1)} %get-tuple-element.30), channel_id=1, source_target_pairs={{0,16},{16,32},{32,48},{48,64},{64,80},{80,96},{96,112},{112,128},... | collective-permute-start | bytes 73736 | tf_op jit(solution)/shard_map/ppermute | solution.py:19
  218.3 26.6 %collective-permute-start.15 = (f32[1,4,8,128]{3,2,1,0:T(8,128)S(1)}, f32[1,4,8,128]{3,2,1,0:T(8,128)S(1)}, u32[]{:S(2)}, u32[]{:S(2)}) collective-permute-start(f32[1,4,8,128]{3,2,1,0:T(8,128)S(1)} %get-tuple-element.11), channel_id=1, source_target_pairs={{1,0},{2,1},{3,2},{4,3},{5,4},{6,5},{7,6},{8,7},{9,8},{10,9},{11,1... | collective-permute-start | bytes 49160 | tf_op jit(solution)/shard_map/ppermute | solution.py:22
  221.9 23.0 %collective-permute-start.14 = (f32[1,4,8,128]{3,2,1,0:T(8,128)S(1)}, f32[1,4,8,128]{3,2,1,0:T(8,128)S(1)}, u32[]{:S(2)}, u32[]{:S(2)}) collective-permute-start(f32[1,4,8,128]{3,2,1,0:T(8,128)S(1)} %get-tuple-element.11), channel_id=1, source_target_pairs={{0,1},{1,2},{2,3},{3,4},{4,5},{5,6},{6,7},{7,8},{8,9},{9,10},{10,1... | collective-permute-start | bytes 49160 | tf_op jit(solution)/shard_map/ppermute | solution.py:19
  224.2 5.3 copy-start.14
  240.2 65.2 %copy-start.6 = (bf16[4,64,8,128]{3,2,1,0:T(8,128)(2,1)S(1)}, bf16[4,64,8,128]{3,2,1,0:T(8,128)(2,1)}, u32[]{:S(2)}) copy-start(bf16[4,64,8,128]{3,2,1,0:T(8,128)(2,1)} %param.21) | copy-start | bytes 1572868
  240.2 65.2 %copy-start.7 = (f32[64,8,128]{2,1,0:T(8,128)S(1)}, f32[64,8,128]{2,1,0:T(8,128)}, u32[]{:S(2)}) copy-start(f32[64,8,128]{2,1,0:T(8,128)} %get-tuple-element.21) | copy-start | bytes 786436
  240.2 65.2 %copy-start.9 = (f32[64,8,128]{2,1,0:T(8,128)S(1)}, f32[64,8,128]{2,1,0:T(8,128)}, u32[]{:S(2)}) copy-start(f32[64,8,128]{2,1,0:T(8,128)} %get-tuple-element.22) | copy-start | bytes 786436
  240.2 65.2 %copy-start.11 = (f32[64,8,128]{2,1,0:T(8,128)S(1)}, f32[64,8,128]{2,1,0:T(8,128)}, u32[]{:S(2)}) copy-start(f32[64,8,128]{2,1,0:T(8,128)} %get-tuple-element.23) | copy-start | bytes 786436
  240.4 62.3 %collective-permute-start.7 = (f32[4,64,4,128]{3,2,1,0:T(4,128)S(1)}, f32[4,64,4,128]{3,2,1,0:T(4,128)S(1)}, u32[]{:S(2)}, u32[]{:S(2)}) collective-permute-start(f32[4,64,4,128]{3,2,1,0:T(4,128)S(1)} %get-tuple-element.20), channel_id=1, source_target_pairs={{16,0},{32,16},{48,32},{64,48},{80,64},{96,80},{112,96},{128,112},... | collective-permute-start | bytes 1572872 | tf_op jit(solution)/shard_map/ppermute | solution.py:22
  241.9 60.9 %collective-permute-start.6 = (f32[4,64,4,128]{3,2,1,0:T(4,128)S(1)}, f32[4,64,4,128]{3,2,1,0:T(4,128)S(1)}, u32[]{:S(2)}, u32[]{:S(2)}) collective-permute-start(f32[4,64,4,128]{3,2,1,0:T(4,128)S(1)} %get-tuple-element.19), channel_id=1, source_target_pairs={{0,16},{16,32},{32,48},{48,64},{64,80},{80,96},{96,112},{112,128},... | collective-permute-start | bytes 1572872 | tf_op jit(solution)/shard_map/ppermute | solution.py:19
  245.0 57.7 %collective-permute-start.17 = (f32[1,12,4,128]{3,2,1,0:T(4,128)S(1)}, f32[1,12,4,128]{3,2,1,0:T(4,128)S(1)}, u32[]{:S(2)}, u32[]{:S(2)}) collective-permute-start(f32[1,12,4,128]{3,2,1,0:T(4,128)S(1)} %get-tuple-element.29), channel_id=1, source_target_pairs={{16,0},{32,16},{48,32},{64,48},{80,64},{96,80},{112,96},{128,112},... | collective-permute-start | bytes 73736 | tf_op jit(solution)/shard_map/ppermute | solution.py:22
  246.3 56.4 %collective-permute-start.16 = (f32[1,12,4,128]{3,2,1,0:T(4,128)S(1)}, f32[1,12,4,128]{3,2,1,0:T(4,128)S(1)}, u32[]{:S(2)}, u32[]{:S(2)}) collective-permute-start(f32[1,12,4,128]{3,2,1,0:T(4,128)S(1)} %get-tuple-element.28), channel_id=1, source_target_pairs={{0,16},{16,32},{32,48},{48,64},{64,80},{80,96},{96,112},{112,128},... | collective-permute-start | bytes 73736 | tf_op jit(solution)/shard_map/ppermute | solution.py:19
  311.8 63.4 %collective-permute-start.13 = (f32[4,64,4,128]{3,2,1,0:T(4,128)S(1)}, f32[4,64,4,128]{3,2,1,0:T(4,128)S(1)}, u32[]{:S(2)}, u32[]{:S(2)}) collective-permute-start(f32[4,64,4,128]{3,2,1,0:T(4,128)S(1)} %get-tuple-element.18), channel_id=1, source_target_pairs={{16,0},{32,16},{48,32},{64,48},{80,64},{96,80},{112,96},{128,112},... | collective-permute-start | bytes 1572872 | tf_op jit(solution)/shard_map/ppermute | solution.py:22
  313.1 62.1 %collective-permute-start.12 = (f32[4,64,4,128]{3,2,1,0:T(4,128)S(1)}, f32[4,64,4,128]{3,2,1,0:T(4,128)S(1)}, u32[]{:S(2)}, u32[]{:S(2)}) collective-permute-start(f32[4,64,4,128]{3,2,1,0:T(4,128)S(1)} %get-tuple-element.17), channel_id=1, source_target_pairs={{0,16},{16,32},{32,48},{48,64},{64,80},{80,96},{96,112},{112,128},... | collective-permute-start | bytes 1572872 | tf_op jit(solution)/shard_map/ppermute | solution.py:19
  318.4 52.3 %collective-permute-start.21 = (f32[1,4,8,128]{3,2,1,0:T(8,128)S(1)}, f32[1,4,8,128]{3,2,1,0:T(8,128)S(1)}, u32[]{:S(2)}, u32[]{:S(2)}) collective-permute-start(f32[1,4,8,128]{3,2,1,0:T(8,128)S(1)} %get-tuple-element.9), channel_id=1, source_target_pairs={{1,0},{2,1},{3,2},{4,3},{5,4},{6,5},{7,6},{8,7},{9,8},{10,9},{11,1... | collective-permute-start | bytes 49160 | tf_op jit(solution)/shard_map/ppermute | solution.py:22
  321.5 49.1 %collective-permute-start.20 = (f32[1,4,8,128]{3,2,1,0:T(8,128)S(1)}, f32[1,4,8,128]{3,2,1,0:T(8,128)S(1)}, u32[]{:S(2)}, u32[]{:S(2)}) collective-permute-start(f32[1,4,8,128]{3,2,1,0:T(8,128)S(1)} %get-tuple-element.9), channel_id=1, source_target_pairs={{0,1},{1,2},{2,3},{3,4},{4,5},{5,6},{6,7},{7,8},{8,9},{9,10},{10,1... | collective-permute-start | bytes 49160 | tf_op jit(solution)/shard_map/ppermute | solution.py:19
  370.7 28.1 %collective-permute-start.23 = (f32[1,12,4,128]{3,2,1,0:T(4,128)S(1)}, f32[1,12,4,128]{3,2,1,0:T(4,128)S(1)}, u32[]{:S(2)}, u32[]{:S(2)}) collective-permute-start(f32[1,12,4,128]{3,2,1,0:T(4,128)S(1)} %get-tuple-element.27), channel_id=1, source_target_pairs={{16,0},{32,16},{48,32},{64,48},{80,64},{96,80},{112,96},{128,112},... | collective-permute-start | bytes 73736 | tf_op jit(solution)/shard_map/ppermute | solution.py:22
  372.0 26.8 %collective-permute-start.22 = (f32[1,12,4,128]{3,2,1,0:T(4,128)S(1)}, f32[1,12,4,128]{3,2,1,0:T(4,128)S(1)}, u32[]{:S(2)}, u32[]{:S(2)}) collective-permute-start(f32[1,12,4,128]{3,2,1,0:T(4,128)S(1)} %get-tuple-element.26), channel_id=1, source_target_pairs={{0,16},{16,32},{32,48},{48,64},{64,80},{80,96},{96,112},{112,128},... | collective-permute-start | bytes 73736 | tf_op jit(solution)/shard_map/ppermute | solution.py:19
  386.1 145.5 %collective-permute-start.19 = (f32[4,64,4,128]{3,2,1,0:T(4,128)}, f32[4,64,4,128]{3,2,1,0:T(4,128)}, u32[]{:S(2)}, u32[]{:S(2)}) collective-permute-start(f32[4,64,4,128]{3,2,1,0:T(4,128)} %get-tuple-element.16), channel_id=1, source_target_pairs={{16,0},{32,16},{48,32},{64,48},{80,64},{96,80},{112,96},{128,112},... | collective-permute-start | bytes 1572872 | tf_op jit(solution)/shard_map/ppermute | solution.py:22
  387.4 144.2 %collective-permute-start.18 = (f32[4,64,4,128]{3,2,1,0:T(4,128)}, f32[4,64,4,128]{3,2,1,0:T(4,128)}, u32[]{:S(2)}, u32[]{:S(2)}) collective-permute-start(f32[4,64,4,128]{3,2,1,0:T(4,128)} %get-tuple-element.15), channel_id=1, source_target_pairs={{0,16},{16,32},{32,48},{48,64},{64,80},{80,96},{96,112},{112,128},... | collective-permute-start | bytes 1572872 | tf_op jit(solution)/shard_map/ppermute | solution.py:19
  475.8 27.9 %copy-start.4 = (f32[4,64,8,128]{3,2,1,0:T(8,128)S(1)}, f32[4,64,8,128]{3,2,1,0:T(8,128)}, u32[]{:S(2)}) copy-start(f32[4,64,8,128]{3,2,1,0:T(8,128)} %copy-done.3) | copy-start | bytes 3145732
  531.5 3.8 copy-start.10
  531.5 3.8 copy-start.12
  531.5 3.8 copy-start.16
  543.9 28.2 %copy-start.18 = (f32[256,4]{1,0:T(8,128)S(1)}, f32[256,4]{1,0:T(8,128)}, u32[]{:S(2)}) copy-start(f32[256,4]{1,0:T(8,128)} %gather_fusion.1) | copy-start | bytes 12292
  543.9 28.2 %copy-start.19 = (f32[256,4]{1,0:T(8,128)S(1)}, f32[256,4]{1,0:T(8,128)}, u32[]{:S(2)}) copy-start(f32[256,4]{1,0:T(8,128)} %gather_fusion.2) | copy-start | bytes 12292
  543.9 202.3 %copy-start.1 = (bf16[4,32,32,128]{3,2,1,0:T(8,128)(2,1)S(1)}, bf16[4,32,32,128]{3,2,1,0:T(8,128)(2,1)}, u32[]{:S(2)}) copy-start(bf16[4,32,32,128]{3,2,1,0:T(8,128)(2,1)} %param.22) | copy-start | bytes 3145732
  (4 other events, 10.9 us)
where the time goes:
time: 748 us; the launch traced here: 746 us
  blocking collectives  355 us (47%)
  starting transfers between devices  126 us (17%)
  local copies, waits for them, and re-layouts  122 us (16%)
  waiting for transfers between devices  84.8 us (11%)
  other arithmetic  52.8 us (7%)
    all_gather x4, blocking collectives, local(): acceleration = lax.all_gather(local_accel, 'dir', axis=0, tiled=True)  181 us
    psum x1, blocking collectives, local(): traces = lax.psum(jnp.stack(records, axis=1), 'tile')  174 us
    ppermute x12, waiting for transfers between devices, padded_2(): lax.ppermute(lax.slice_in_dim(block, 0, width, axis=dim), axis, backward)  67.6 us
    add x4, local copies, waits for them, and re-layouts, local(): 2.0 * current_born - earlier_born  64.7 us
    ppermute x12, starting transfers between devices, padded_2(): lax.ppermute(lax.slice_in_dim(block, block.shape[dim] - width, None, axis...  54.4 us
    ppermute x12, starting transfers between devices, padded_2(): lax.ppermute(lax.slice_in_dim(block, 0, width, axis=dim), axis, backward)  48.9 us
    gather x4, local copies, waits for them, and re-layouts, local(): jnp.take(following.reshape(following.shape[0], -1), flat_index, axis=1)  46.3 us
    add x4, other arithmetic, local(): 2.0 * current_born - earlier_born  28.4 us
  transfers between devices with their start and end apart: 26, of which 4 were waited for; matrix products, arithmetic and copies ran while one was open for 17% of the time, Pallas kernels for 0%

commit v1 on v0

--- a/solution.py
+++ b/solution.py
@@ -133,7 +133,16 @@
         local_accel = operate(
             jnp.pad(back_wide[0], ((0, 0), (0, 0), (4, 4))), slab_stiff, slab_drift
         )
-        acceleration = lax.all_gather(local_accel, "dir", axis=0, tiled=True)
+
+        def things_launch(local_array):
+            return jnp.concatenate(
+                lax.all_to_all(
+                    jnp.stack([local_array] * lax.axis_size("dir"), axis=0), "dir", 0, 0
+                ),
+                axis=0,
+            )
+
+        acceleration = things_launch(local_accel)
         previous, present = (
             present,
             2.0 * present - previous + local_accel + wavelet[step_index] * source_mask,

time: 748 us -> 723 us (0.967)
  blocking collectives: 355 us -> 172 us
  other arithmetic: 52.8 us -> 143 us
  starting transfers between devices: 126 us -> 181 us
  waiting for transfers between devices: 84.8 us -> 92.9 us
    all_gather x4 -> x0, blocking collectives: 181 us -> none  [local(): acceleration = lax.all_gather(local_accel, 'dir', axis=0, tiled=True)]
    add x4, other arithmetic: 28.4 us -> 114 us  [local(): 2.0 * current_born - earlier_born]
    all_to_all x0 -> x4, starting transfers between devices: none -> 30.6 us  [things_launch(): lax.all_to_all(jnp.stack([local_array] * lax.axis_size('dir'), axis=0), '...]
    ppermute x12, starting transfers between devices: 54.4 us -> 70.3 us  [padded_2(): lax.ppermute(lax.slice_in_dim(block, block.shape[dim] - width, None, axis...]
    ppermute x12, starting transfers between devices: 48.9 us -> 57.5 us  [padded_2(): lax.ppermute(lax.slice_in_dim(block, 0, width, axis=dim), axis, backward)]
  transfers between devices with their start and end apart: 26 -> 30, of which waited for: 4 -> 8; matrix products, arithmetic and copies ran while one was open for 17% -> 17% of each run, Pallas kernels for 0% -> 0%
where the time goes in v1:
time: 723 us; the launch traced here: 721 us
  starting transfers between devices  181 us (25%)
  blocking collectives  172 us (24%)
  other arithmetic  143 us (20%)
  local copies, waits for them, and re-layouts  126 us (17%)
  waiting for transfers between devices  92.9 us (13%)
    psum x1, blocking collectives, local(): traces = lax.psum(jnp.stack(records, axis=1), 'tile')  172 us
    add x4, other arithmetic, local(): 2.0 * current_born - earlier_born  114 us
    ppermute x12, starting transfers between devices, padded_2(): lax.ppermute(lax.slice_in_dim(block, block.shape[dim] - width, None, axis...  70.3 us
    ppermute x12, waiting for transfers between devices, padded_2(): lax.ppermute(lax.slice_in_dim(block, 0, width, axis=dim), axis, backward)  68.5 us
    add x4, local copies, waits for them, and re-layouts, local(): 2.0 * current_born - earlier_born  64.7 us
    ppermute x12, starting transfers between devices, padded_2(): lax.ppermute(lax.slice_in_dim(block, 0, width, axis=dim), axis, backward)  57.5 us
    gather x4, local copies, waits for them, and re-layouts, local(): jnp.take(following.reshape(following.shape[0], -1), flat_index, axis=1)  46.3 us
    all_to_all x4, starting transfers between devices, things_launch(): lax.all_to_all(jnp.stack([local_array] * lax.axis_size('dir'), axis=0), '...  30.6 us
  transfers between devices with their start and end apart: 30, of which 8 were waited for; matrix products, arithmetic and copies ran while one was open for 17% of the time, Pallas kernels for 0%

profile of v1, /device:TPU:24, one launch (start us, length us, event | category | flops | bytes accessed | tf_op | source)
XLA Modules:
  0.0 720.9 jit_solution(7517748783054560155)
XLA Ops:
  3.8 17.9 %all-to-all-start = ((bf16[1,32,2]{2,0,1:T(2,128)(2,1)}), bf16[1,32,2]{2,0,1:T(2,128)(2,1)S(1)}, u32[]{:S(2)}, u32[]{:S(2)}) async-start(bf16[1,32,2]{2,0,1:T(2,128)(2,1)} %all_to_all.28), calls=%async_computation | async-start | bytes 32768 | tf_op jit(solution)/shard_map/all_to_all | solution.py:74
  22.6 2.7 copy.42
  25.3 10.9 %all-to-all-done = bf16[1,32,2]{2,0,1:T(2,128)(2,1)S(1)} async-done(((bf16[1,32,2]{2,0,1:T(2,128)(2,1)}), bf16[1,32,2]{2,0,1:T(2,128)(2,1)S(1)}, u32[]{:S(2)}, u32[]{:S(2)}) %all-to-all-start) | async-done | bytes 160 | tf_op jit(solution)/shard_map/all_to_all | solution.py:74
  36.3 4.8 all-to-all-start.1
  41.8 4.0 collective-permute-start.3
  45.8 1.9 collective-permute-start.2
  50.2 3.1 collective-permute-start
  56.9 68.5 %collective-permute-done.3 = f32[1,4,8,128]{3,2,1,0:T(8,128)S(1)} collective-permute-done((f32[1,4,8,128]{3,2,1,0:T(8,128)S(1)}, f32[1,4,8,128]{3,2,1,0:T(8,128)S(1)}, u32[]{:S(2)}, u32[]{:S(2)}) %collective-permute-start.3) | collective-permute-done | bytes 16416 | tf_op jit(solution)/shard_map/ppermute | solution.py:22
  126.7 3.0 collective-permute-start.4
  130.6 1.5 fusion.39
  132.1 27.6 %collective-permute-start.9 = (f32[1,4,8,128]{3,2,1,0:T(8,128)S(1)}, f32[1,4,8,128]{3,2,1,0:T(8,128)S(1)}, u32[]{:S(2)}, u32[]{:S(2)}) collective-permute-start(f32[1,4,8,128]{3,2,1,0:T(8,128)S(1)} %bitcast.140), channel_id=1, source_target_pairs={{1,0},{2,1},{3,2},{4,3},{5,4},{6,5},{7,6},{8,7},{9,8},{10,9},{11,1... | collective-permute-start | bytes 49160 | tf_op jit(solution)/shard_map/ppermute | solution.py:22
  159.8 1.9 collective-permute-start.8
  161.8 6.3 collective-permute-done.8
  169.4 10.4 %collective-permute-start.10 = (f32[1,12,4,128]{3,2,1,0:T(4,128)S(1)}, f32[1,12,4,128]{3,2,1,0:T(4,128)S(1)}, u32[]{:S(2)}, u32[]{:S(2)}) collective-permute-start(f32[1,12,4,128]{3,2,1,0:T(4,128)S(1)} %get-tuple-element.30), channel_id=1, source_target_pairs={{0,16},{16,32},{32,48},{48,64},{64,80},{80,96},{96,112},{112,128},... | collective-permute-start | bytes 73736 | tf_op jit(solution)/shard_map/ppermute | solution.py:19
  181.3 4.5 all-to-all-start.2
  185.9 4.1 select_maximum_fusion.6
  190.0 2.8 fusion.6
  193.0 28.5 %multiply_add_fusion.3 = f32[4,64,8,128]{3,2,1,0:T(8,128)S(1)} fusion(f32[4,64,8,128]{3,2,1,0:T(8,128)S(1)} %bitcast.136, f32[4,72,16,136]{3,2,1,0:T(8,128)} %select_maximum_fusion.6, f32[4,64,4,128]{3,2,1,0:T(4,128)} %copy-done.6, f32[4,64,8,128]{3,2,1,0:T(8,128)S(1)} %convert_element_type.62, f32[4,64,4,128]{3,2,1,0:T(4,128)} %copy-done.7, ...), kind=kLoop, calls=%fused_computation.110 | loop fusion | flops 23855104 | bytes 22806528 | tf_op jit(solution)/shard_map/add | solution.py:152
  223.9 7.9 %collective-permute-start.6 = (f32[4,64,4,128]{3,2,1,0:T(4,128)}, f32[4,64,4,128]{3,2,1,0:T(4,128)S(1)}, u32[]{:S(2)}, u32[]{:S(2)}) collective-permute-start(f32[4,64,4,128]{3,2,1,0:T(4,128)} %get-tuple-element.19), channel_id=1, source_target_pairs={{0,16},{16,32},{32,48},{48,64},{64,80},{80,96},{96,112},{112,128},... | collective-permute-start | bytes 1572872 | tf_op jit(solution)/shard_map/ppermute | solution.py:19
  231.8 1.5 fusion.108
  233.3 5.3 collective-permute-start.15
  238.6 1.9 collective-permute-start.14
  241.3 8.7 %all-to-all-start.3 = ((f32[16,4,8,128]{3,2,1,0:T(8,128)}), f32[16,4,8,128]{3,2,1,0:T(8,128)}, u32[]{:S(2)}, u32[]{:S(2)}) async-start(f32[16,4,8,128]{3,2,1,0:T(8,128)} %stack.19), calls=%async_computation.3 | async-start | bytes 524288 | tf_op jit(solution)/shard_map/all_to_all | solution.py:139
  251.4 8.3 %collective-permute-start.16 = (f32[1,12,4,128]{3,2,1,0:T(4,128)S(1)}, f32[1,12,4,128]{3,2,1,0:T(4,128)S(1)}, u32[]{:S(2)}, u32[]{:S(2)}) collective-permute-start(f32[1,12,4,128]{3,2,1,0:T(4,128)S(1)} %get-tuple-element.28), channel_id=1, source_target_pairs={{0,16},{16,32},{32,48},{48,64},{64,80},{80,96},{96,112},{112,128},... | collective-permute-start | bytes 73736 | tf_op jit(solution)/shard_map/ppermute | solution.py:19
  261.2 4.1 select_maximum_fusion.4
  265.3 4.8 all-to-all-done.3
  270.1 28.1 %multiply_add_fusion.2 = f32[4,64,8,128]{3,2,1,0:T(8,128)S(1)} fusion(f32[4,64,8,128]{3,2,1,0:T(8,128)S(1)} %bitcast.137, f32[4,72,16,136]{3,2,1,0:T(8,128)} %select_maximum_fusion.4, f32[4,64,4,128]{3,2,1,0:T(4,128)} %copy-done.8, f32[4,64,8,128]{3,2,1,0:T(8,128)S(1)} %multiply_add_fusion.3, f32[4,64,4,128]{3,2,1,0:T(4,128)} %copy-done.9, ...), kind=kLoop, calls=%fused_computation.109 | loop fusion | flops 23855104 | bytes 22806528 | tf_op jit(solution)/shard_map/add | solution.py:152
  300.7 9.4 %collective-permute-start.12 = (f32[4,64,4,128]{3,2,1,0:T(4,128)}, f32[4,64,4,128]{3,2,1,0:T(4,128)}, u32[]{:S(2)}, u32[]{:S(2)}) collective-permute-start(f32[4,64,4,128]{3,2,1,0:T(4,128)} %get-tuple-element.17), channel_id=1, source_target_pairs={{0,16},{16,32},{32,48},{48,64},{64,80},{80,96},{96,112},{112,128},... | collective-permute-start | bytes 1572872 | tf_op jit(solution)/shard_map/ppermute | solution.py:19
  310.1 2.1 fusion.42
  312.2 10.2 %collective-permute-start.21 = (f32[1,4,8,128]{3,2,1,0:T(8,128)S(1)}, f32[1,4,8,128]{3,2,1,0:T(8,128)S(1)}, u32[]{:S(2)}, u32[]{:S(2)}) collective-permute-start(f32[1,4,8,128]{3,2,1,0:T(8,128)S(1)} %get-tuple-element.9), channel_id=1, source_target_pairs={{1,0},{2,1},{3,2},{4,3},{5,4},{6,5},{7,6},{8,7},{9,8},{10,9},{11,1... | collective-permute-start | bytes 49160 | tf_op jit(solution)/shard_map/ppermute | solution.py:22
  322.4 1.9 collective-permute-start.20
  325.1 8.7 %all-to-all-start.4 = ((f32[16,4,8,128]{3,2,1,0:T(8,128)}), f32[16,4,8,128]{3,2,1,0:T(8,128)}, u32[]{:S(2)}, u32[]{:S(2)}) async-start(f32[16,4,8,128]{3,2,1,0:T(8,128)} %stack.20), calls=%async_computation.4 | async-start | bytes 524288 | tf_op jit(solution)/shard_map/all_to_all | solution.py:139
  335.1 11.4 %collective-permute-start.22 = (f32[1,12,4,128]{3,2,1,0:T(4,128)S(1)}, f32[1,12,4,128]{3,2,1,0:T(4,128)S(1)}, u32[]{:S(2)}, u32[]{:S(2)}) collective-permute-start(f32[1,12,4,128]{3,2,1,0:T(4,128)S(1)} %get-tuple-element.26), channel_id=1, source_target_pairs={{0,16},{16,32},{32,48},{48,64},{64,80},{80,96},{96,112},{112,128},... | collective-permute-start | bytes 73736 | tf_op jit(solution)/shard_map/ppermute | solution.py:19
  347.4 5.1 select_maximum_fusion.2
  352.6 28.0 %multiply_add_fusion.1 = f32[4,64,8,128]{3,2,1,0:T(8,128)S(1)} fusion(f32[4,64,8,128]{3,2,1,0:T(8,128)S(1)} %bitcast.138, f32[4,72,16,136]{3,2,1,0:T(8,128)} %select_maximum_fusion.2, f32[4,64,4,128]{3,2,1,0:T(4,128)} %collective-permute-done.13, f32[4,64,8,128]{3,2,1,0:T(8,128)S(1)} %multiply_add_fusion.2, f32[4,64,4,128]{3,2,1,0:T(4,128)} %collective-permute-done.12, ...), kind=kLoop, calls=%fused_computation.108 | loop fusion | flops 23592960 | bytes 23330816 | tf_op jit(solution)/shard_map/add | solution.py:152
  384.0 9.1 %collective-permute-start.18 = (f32[4,64,4,128]{3,2,1,0:T(4,128)}, f32[4,64,4,128]{3,2,1,0:T(4,128)}, u32[]{:S(2)}, u32[]{:S(2)}) collective-permute-start(f32[4,64,4,128]{3,2,1,0:T(4,128)} %get-tuple-element.15), channel_id=1, source_target_pairs={{0,16},{16,32},{32,48},{48,64},{64,80},{80,96},{96,112},{112,128},... | collective-permute-start | bytes 1572872 | tf_op jit(solution)/shard_map/ppermute | solution.py:19
  394.7 8.7 %all-to-all-start.5 = ((f32[16,4,8,128]{3,2,1,0:T(8,128)}), f32[16,4,8,128]{3,2,1,0:T(8,128)}, u32[]{:S(2)}, u32[]{:S(2)}) async-start(f32[16,4,8,128]{3,2,1,0:T(8,128)} %stack.21), calls=%async_computation.5 | async-start | bytes 524288 | tf_op jit(solution)/shard_map/all_to_all | solution.py:139
  403.4 16.0 %copy.45 = f32[4,64,8,128]{0,3,2,1:T(8,128)} copy(f32[4,64,8,128]{3,2,1,0:T(8,128)S(1)} %multiply_add_fusion.3) | data formatting | bytes 2097152 | tf_op jit(solution)/shard_map/add | solution.py:152
  419.4 11.3 %gather_fusion = f32[256,4]{1,0:T(8,128)S(1)} fusion(f32[4,65536]{0,1:T(8,128)} %bitcast.132, s32[1024]{0:T(1024)S(1)} %pad_clamp_fusion), kind=kCustom, calls=%fused_computation.clone | custom fusion | bytes 9216 | tf_op jit(solution)/shard_map/jit(_take)/gather | solution.py:158
  430.7 16.0 %copy.46 = f32[4,64,8,128]{0,3,2,1:T(8,128)} copy(f32[4,64,8,128]{3,2,1,0:T(8,128)S(1)} %multiply_add_fusion.2) | data formatting | bytes 2097152 | tf_op jit(solution)/shard_map/add | solution.py:152
  446.6 11.9 %gather_fusion.1 = f32[256,4]{1,0:T(8,128)} fusion(f32[4,65536]{0,1:T(8,128)} %bitcast.134, s32[1024]{0:T(1024)S(1)} %pad_clamp_fusion), kind=kCustom, calls=%fused_computation.1.clone | custom fusion | bytes 9216 | tf_op jit(solution)/shard_map/jit(_take)/gather | solution.py:158
  458.5 15.9 %copy.47 = f32[4,64,8,128]{0,3,2,1:T(8,128)} copy(f32[4,64,8,128]{3,2,1,0:T(8,128)S(1)} %copy-done.3) | data formatting | bytes 2097152 | tf_op jit(solution)/shard_map/add | solution.py:152
  474.5 11.9 %gather_fusion.2 = f32[256,4]{1,0:T(8,128)} fusion(f32[4,65536]{0,1:T(8,128)} %bitcast.135, s32[1024]{0:T(1024)S(1)} %pad_clamp_fusion), kind=kCustom, calls=%fused_computation.2.clone | custom fusion | bytes 9216 | tf_op jit(solution)/shard_map/jit(_take)/gather | solution.py:158
  486.4 5.1 select_maximum_fusion
  491.5 29.0 %multiply_add_fusion = f32[4,64,8,128]{3,2,1,0:T(8,128)} fusion(f32[4,64,8,128]{3,2,1,0:T(8,128)S(1)} %bitcast.139, f32[4,72,16,136]{3,2,1,0:T(8,128)} %select_maximum_fusion, f32[4,64,4,128]{3,2,1,0:T(4,128)} %collective-permute-done.19, f32[4,64,8,128]{3,2,1,0:T(8,128)S(1)} %copy-done.3, f32[4,64,4,128]{3,2,1,0:T(4,128)} %collective-permute-done.18, ...), kind=kLoop, calls=%fused_computation.107 | loop fusion | flops 23592960 | bytes 23330816 | tf_op jit(solution)/shard_map/add | solution.py:152
  520.5 16.9 %copy.48 = f32[4,64,8,128]{0,3,2,1:T(8,128)} copy(f32[4,64,8,128]{3,2,1,0:T(8,128)} %multiply_add_fusion) | data formatting | bytes 2097152 | tf_op jit(solution)/shard_map/add | solution.py:152
  537.4 11.3 %gather_fusion.3 = f32[256,4]{1,0:T(8,128)S(1)} fusion(f32[4,65536]{0,1:T(8,128)} %bitcast.133, s32[1024]{0:T(1024)S(1)} %pad_clamp_fusion), kind=kCustom, calls=%fused_computation.3.clone | custom fusion | bytes 9216 | tf_op jit(solution)/shard_map/jit(_take)/gather | solution.py:158
  549.2 171.8 %psum.7 = f32[4,4,256]{2,1,0:T(4,128)} all-reduce(f32[4,4,256]{2,1,0:T(4,128)S(1)} %pad_maximum_fusion.12), channel_id=1, replica_groups=mesh['tile'=32,'dir'=16] {'tile'}, use_global_device_ids=true, to_apply=%region_1.3 | all-reduce | flops 4096 | bytes 32768 | tf_op jit(solution)/shard_map/psum | solution.py:162
  (137 shorter events, 32.7 us)
Async XLA Ops:
  3.8 32.4 %all-to-all-start = ((bf16[1,32,2]{2,0,1:T(2,128)(2,1)}), bf16[1,32,2]{2,0,1:T(2,128)(2,1)S(1)}, u32[]{:S(2)}, u32[]{:S(2)}) async-start(bf16[1,32,2]{2,0,1:T(2,128)(2,1)} %all_to_all.28), calls=%async_computation | async-start | bytes 32768 | tf_op jit(solution)/shard_map/all_to_all | solution.py:74
  22.6 30.6 %copy-start.10 = (bf16[3,64,8,128]{3,2,1,0:T(8,128)(2,1)S(1)}, bf16[3,64,8,128]{3,2,1,0:T(8,128)(2,1)}, u32[]{:S(2)}) copy-start(bf16[3,64,8,128]{3,2,1,0:T(8,128)(2,1)} %param.19) | copy-start | bytes 1179652
  25.3 28.0 %copy-start.16 = (s32[3]{0:T(128)S(1)}, s32[3]{0:T(128)}, u32[]{:S(2)}) copy-start(s32[3]{0:T(128)} %param.26) | copy-start | bytes 40
  25.3 30.9 %copy-start.17 = (f32[4]{0:T(128)S(1)}, f32[4]{0:T(128)}, u32[]{:S(2)}) copy-start(f32[4]{0:T(128)} %param.25) | copy-start | bytes 52
  25.3 105.0 %copy-start.13 = (bf16[64,8,128]{2,1,0:T(8,128)(2,1)S(1)}, bf16[64,8,128]{2,1,0:T(8,128)(2,1)}, u32[]{:S(2)}) copy-start(bf16[64,8,128]{2,1,0:T(8,128)(2,1)} %param.18) | copy-start | bytes 393220
  36.3 144.4 %all-to-all-start.1 = ((bf16[4,64,32,128]{3,2,0,1:T(8,128)(2,1)}), bf16[4,64,32,128]{3,2,0,1:T(8,128)(2,1)}, u32[]{:S(2)}, u32[]{:S(2)}) async-start(bf16[4,64,32,128]{3,2,0,1:T(8,128)(2,1)} %copy.42), calls=%async_computation.1 | async-start | bytes 4194304 | tf_op jit(solution)/shard_map/all_to_all | solution.py:73
  41.8 83.6 %collective-permute-start.3 = (f32[1,4,8,128]{3,2,1,0:T(8,128)S(1)}, f32[1,4,8,128]{3,2,1,0:T(8,128)S(1)}, u32[]{:S(2)}, u32[]{:S(2)}) collective-permute-start(f32[1,4,8,128]{3,2,1,0:T(8,128)S(1)} %dynamic-slice_bitcast_fusion.3), channel_id=1, source_target_pairs={{1,0},{2,1},{3,2},{4,3},{5,4},{6,5},{7,6},{8,7},{9,8},{10,9},{11,1... | collective-permute-start | bytes 49160 | tf_op jit(solution)/shard_map/ppermute | solution.py:22
  45.8 79.6 %collective-permute-start.2 = (f32[1,4,8,128]{3,2,1,0:T(8,128)S(1)}, f32[1,4,8,128]{3,2,1,0:T(8,128)S(1)}, u32[]{:S(2)}, u32[]{:S(2)}) collective-permute-start(f32[1,4,8,128]{3,2,1,0:T(8,128)S(1)} %dynamic-slice_bitcast_fusion.3), channel_id=1, source_target_pairs={{0,1},{1,2},{2,3},{3,4},{4,5},{5,6},{6,7},{7,8},{8,9},{9,10},{10,1... | collective-permute-start | bytes 49160 | tf_op jit(solution)/shard_map/ppermute | solution.py:19
  48.9 137.0 %collective-permute-start.1 = (f32[4,64,4,128]{3,2,1,0:T(4,128)}, f32[4,64,4,128]{3,2,1,0:T(4,128)S(1)}, u32[]{:S(2)}, u32[]{:S(2)}) collective-permute-start(f32[4,64,4,128]{3,2,1,0:T(4,128)} %get-tuple-element.25), channel_id=1, source_target_pairs={{16,0},{32,16},{48,32},{64,48},{80,64},{96,80},{112,96},{128,112},... | collective-permute-start | bytes 1572872 | tf_op jit(solution)/shard_map/ppermute | solution.py:22
  50.2 135.7 %collective-permute-start = (f32[4,64,4,128]{3,2,1,0:T(4,128)}, f32[4,64,4,128]{3,2,1,0:T(4,128)S(1)}, u32[]{:S(2)}, u32[]{:S(2)}) collective-permute-start(f32[4,64,4,128]{3,2,1,0:T(4,128)} %get-tuple-element.24), channel_id=1, source_target_pairs={{0,16},{16,32},{32,48},{48,64},{64,80},{80,96},{96,112},{112,128},... | collective-permute-start | bytes 1572872 | tf_op jit(solution)/shard_map/ppermute | solution.py:19
  53.3 108.4 %copy-start.5 = (f32[3,64,8,128]{3,2,1,0:T(8,128)}, f32[3,64,8,128]{3,2,1,0:T(8,128)S(1)}, u32[]{:S(2)}) copy-start(f32[3,64,8,128]{3,2,1,0:T(8,128)S(1)} %convert_element_type.65) | copy-start | bytes 2359300
  55.4 106.4 %copy-start.18 = (pred[4,8]{1,0:T(4,128)(4,1)}, pred[4,8]{1,0:T(4,128)(4,1)S(1)}, u32[]{:S(2)}) copy-start(pred[4,8]{1,0:T(4,128)(4,1)S(1)} %broadcast_and_fusion) | copy-start | bytes 100
  125.4 5.0 collective-permute-start.5
  126.7 3.9 collective-permute-start.4
  130.3 31.5 %copy-start.21 = (pred[128]{0:T(512)(128)(4,1)}, pred[128]{0:T(512)(128)(4,1)S(1)}, u32[]{:S(2)}) copy-start(pred[128]{0:T(512)(128)(4,1)S(1)} %iota_compare_fusion.7) | copy-start | bytes 388
  132.1 29.7 %collective-permute-start.9 = (f32[1,4,8,128]{3,2,1,0:T(8,128)S(1)}, f32[1,4,8,128]{3,2,1,0:T(8,128)S(1)}, u32[]{:S(2)}, u32[]{:S(2)}) collective-permute-start(f32[1,4,8,128]{3,2,1,0:T(8,128)S(1)} %bitcast.140), channel_id=1, source_target_pairs={{1,0},{2,1},{3,2},{4,3},{5,4},{6,5},{7,6},{8,7},{9,8},{10,9},{11,1... | collective-permute-start | bytes 49160 | tf_op jit(solution)/shard_map/ppermute | solution.py:22
  159.8 8.3 %collective-permute-start.8 = (f32[1,4,8,128]{3,2,1,0:T(8,128)S(1)}, f32[1,4,8,128]{3,2,1,0:T(8,128)S(1)}, u32[]{:S(2)}, u32[]{:S(2)}) collective-permute-start(f32[1,4,8,128]{3,2,1,0:T(8,128)S(1)} %bitcast.141), channel_id=1, source_target_pairs={{0,1},{1,2},{2,3},{3,4},{4,5},{5,6},{6,7},{7,8},{8,9},{9,10},{10,1... | collective-permute-start | bytes 49160 | tf_op jit(solution)/shard_map/ppermute | solution.py:19
  168.1 11.8 %collective-permute-start.11 = (f32[1,12,4,128]{3,2,1,0:T(4,128)S(1)}, f32[1,12,4,128]{3,2,1,0:T(4,128)S(1)}, u32[]{:S(2)}, u32[]{:S(2)}) collective-permute-start(f32[1,12,4,128]{3,2,1,0:T(4,128)S(1)} %get-tuple-element.31), channel_id=1, source_target_pairs={{16,0},{32,16},{48,32},{64,48},{80,64},{96,80},{112,96},{128,112},... | collective-permute-start | bytes 73736 | tf_op jit(solution)/shard_map/ppermute | solution.py:22
  169.4 11.2 %collective-permute-start.10 = (f32[1,12,4,128]{3,2,1,0:T(4,128)S(1)}, f32[1,12,4,128]{3,2,1,0:T(4,128)S(1)}, u32[]{:S(2)}, u32[]{:S(2)}) collective-permute-start(f32[1,12,4,128]{3,2,1,0:T(4,128)S(1)} %get-tuple-element.30), channel_id=1, source_target_pairs={{0,16},{16,32},{32,48},{48,64},{64,80},{80,96},{96,112},{112,128},... | collective-permute-start | bytes 73736 | tf_op jit(solution)/shard_map/ppermute | solution.py:19
  181.3 11.6 %all-to-all-start.2 = ((f32[16,4,8,128]{3,2,1,0:T(8,128)}), f32[16,4,8,128]{3,2,1,0:T(8,128)}, u32[]{:S(2)}, u32[]{:S(2)}) async-start(f32[16,4,8,128]{3,2,1,0:T(8,128)} %stack.18), calls=%async_computation.2 | async-start | bytes 524288 | tf_op jit(solution)/shard_map/all_to_all | solution.py:139
  192.9 38.8 %copy-start.19 = (pred[4,8]{1,0:T(4,128)(4,1)S(1)}, pred[4,8]{1,0:T(4,128)(4,1)}, u32[]{:S(2)}) copy-start(pred[4,8]{1,0:T(4,128)(4,1)} %copy-done.18) | copy-start | bytes 100
  193.0 38.8 %copy-start.22 = (pred[128]{0:T(512)(128)(4,1)S(1)}, pred[128]{0:T(512)(128)(4,1)}, u32[]{:S(2)}) copy-start(pred[128]{0:T(512)(128)(4,1)} %copy-done.21) | copy-start | bytes 388
  222.6 38.5 %collective-permute-start.7 = (f32[4,64,4,128]{3,2,1,0:T(4,128)}, f32[4,64,4,128]{3,2,1,0:T(4,128)S(1)}, u32[]{:S(2)}, u32[]{:S(2)}) collective-permute-start(f32[4,64,4,128]{3,2,1,0:T(4,128)} %get-tuple-element.20), channel_id=1, source_target_pairs={{16,0},{32,16},{48,32},{64,48},{80,64},{96,80},{112,96},{128,112},... | collective-permute-start | bytes 1572872 | tf_op jit(solution)/shard_map/ppermute | solution.py:22
  223.9 37.3 %collective-permute-start.6 = (f32[4,64,4,128]{3,2,1,0:T(4,128)}, f32[4,64,4,128]{3,2,1,0:T(4,128)S(1)}, u32[]{:S(2)}, u32[]{:S(2)}) collective-permute-start(f32[4,64,4,128]{3,2,1,0:T(4,128)} %get-tuple-element.19), channel_id=1, source_target_pairs={{0,16},{16,32},{32,48},{48,64},{64,80},{80,96},{96,112},{112,128},... | collective-permute-start | bytes 1572872 | tf_op jit(solution)/shard_map/ppermute | solution.py:19
  233.3 16.7 %collective-permute-start.15 = (f32[1,4,8,128]{3,2,1,0:T(8,128)S(1)}, f32[1,4,8,128]{3,2,1,0:T(8,128)S(1)}, u32[]{:S(2)}, u32[]{:S(2)}) collective-permute-start(f32[1,4,8,128]{3,2,1,0:T(8,128)S(1)} %get-tuple-element.11), channel_id=1, source_target_pairs={{1,0},{2,1},{3,2},{4,3},{5,4},{6,5},{7,6},{8,7},{9,8},{10,9},{11,1... | collective-permute-start | bytes 49160 | tf_op jit(solution)/shard_map/ppermute | solution.py:22
  238.6 11.4 %collective-permute-start.14 = (f32[1,4,8,128]{3,2,1,0:T(8,128)S(1)}, f32[1,4,8,128]{3,2,1,0:T(8,128)S(1)}, u32[]{:S(2)}, u32[]{:S(2)}) collective-permute-start(f32[1,4,8,128]{3,2,1,0:T(8,128)S(1)} %get-tuple-element.11), channel_id=1, source_target_pairs={{0,1},{1,2},{2,3},{3,4},{4,5},{5,6},{6,7},{7,8},{8,9},{9,10},{10,1... | collective-permute-start | bytes 49160 | tf_op jit(solution)/shard_map/ppermute | solution.py:19
  241.3 28.8 %all-to-all-start.3 = ((f32[16,4,8,128]{3,2,1,0:T(8,128)}), f32[16,4,8,128]{3,2,1,0:T(8,128)}, u32[]{:S(2)}, u32[]{:S(2)}) async-start(f32[16,4,8,128]{3,2,1,0:T(8,128)} %stack.19), calls=%async_computation.3 | async-start | bytes 524288 | tf_op jit(solution)/shard_map/all_to_all | solution.py:139
  250.1 9.6 %collective-permute-start.17 = (f32[1,12,4,128]{3,2,1,0:T(4,128)S(1)}, f32[1,12,4,128]{3,2,1,0:T(4,128)S(1)}, u32[]{:S(2)}, u32[]{:S(2)}) collective-permute-start(f32[1,12,4,128]{3,2,1,0:T(4,128)S(1)} %get-tuple-element.29), channel_id=1, source_target_pairs={{16,0},{32,16},{48,32},{64,48},{80,64},{96,80},{112,96},{128,112},... | collective-permute-start | bytes 73736 | tf_op jit(solution)/shard_map/ppermute | solution.py:22
  251.4 9.0 %collective-permute-start.16 = (f32[1,12,4,128]{3,2,1,0:T(4,128)S(1)}, f32[1,12,4,128]{3,2,1,0:T(4,128)S(1)}, u32[]{:S(2)}, u32[]{:S(2)}) collective-permute-start(f32[1,12,4,128]{3,2,1,0:T(4,128)S(1)} %get-tuple-element.28), channel_id=1, source_target_pairs={{0,16},{16,32},{32,48},{48,64},{64,80},{80,96},{96,112},{112,128},... | collective-permute-start | bytes 73736 | tf_op jit(solution)/shard_map/ppermute | solution.py:19
  270.1 39.9 %copy-start.20 = (pred[4,8]{1,0:T(4,128)(4,1)S(1)}, pred[4,8]{1,0:T(4,128)(4,1)}, u32[]{:S(2)}) copy-start(pred[4,8]{1,0:T(4,128)(4,1)} %copy-done.18) | copy-start | bytes 100
  270.1 39.9 %copy-start.23 = (pred[128]{0:T(512)(128)(4,1)S(1)}, pred[128]{0:T(512)(128)(4,1)}, u32[]{:S(2)}) copy-start(pred[128]{0:T(512)(128)(4,1)} %copy-done.21) | copy-start | bytes 388
  299.4 48.0 %collective-permute-start.13 = (f32[4,64,4,128]{3,2,1,0:T(4,128)}, f32[4,64,4,128]{3,2,1,0:T(4,128)}, u32[]{:S(2)}, u32[]{:S(2)}) collective-permute-start(f32[4,64,4,128]{3,2,1,0:T(4,128)} %get-tuple-element.18), channel_id=1, source_target_pairs={{16,0},{32,16},{48,32},{64,48},{80,64},{96,80},{112,96},{128,112},... | collective-permute-start | bytes 1572872 | tf_op jit(solution)/shard_map/ppermute | solution.py:22
  300.7 46.7 %collective-permute-start.12 = (f32[4,64,4,128]{3,2,1,0:T(4,128)}, f32[4,64,4,128]{3,2,1,0:T(4,128)}, u32[]{:S(2)}, u32[]{:S(2)}) collective-permute-start(f32[4,64,4,128]{3,2,1,0:T(4,128)} %get-tuple-element.17), channel_id=1, source_target_pairs={{0,16},{16,32},{32,48},{48,64},{64,80},{80,96},{96,112},{112,128},... | collective-permute-start | bytes 1572872 | tf_op jit(solution)/shard_map/ppermute | solution.py:19
  312.2 21.6 %collective-permute-start.21 = (f32[1,4,8,128]{3,2,1,0:T(8,128)S(1)}, f32[1,4,8,128]{3,2,1,0:T(8,128)S(1)}, u32[]{:S(2)}, u32[]{:S(2)}) collective-permute-start(f32[1,4,8,128]{3,2,1,0:T(8,128)S(1)} %get-tuple-element.9), channel_id=1, source_target_pairs={{1,0},{2,1},{3,2},{4,3},{5,4},{6,5},{7,6},{8,7},{9,8},{10,9},{11,1... | collective-permute-start | bytes 49160 | tf_op jit(solution)/shard_map/ppermute | solution.py:22
  322.4 11.3 %collective-permute-start.20 = (f32[1,4,8,128]{3,2,1,0:T(8,128)S(1)}, f32[1,4,8,128]{3,2,1,0:T(8,128)S(1)}, u32[]{:S(2)}, u32[]{:S(2)}) collective-permute-start(f32[1,4,8,128]{3,2,1,0:T(8,128)S(1)} %get-tuple-element.9), channel_id=1, source_target_pairs={{0,1},{1,2},{2,3},{3,4},{4,5},{5,6},{6,7},{7,8},{8,9},{9,10},{10,1... | collective-permute-start | bytes 49160 | tf_op jit(solution)/shard_map/ppermute | solution.py:19
  325.1 27.5 %all-to-all-start.4 = ((f32[16,4,8,128]{3,2,1,0:T(8,128)}), f32[16,4,8,128]{3,2,1,0:T(8,128)}, u32[]{:S(2)}, u32[]{:S(2)}) async-start(f32[16,4,8,128]{3,2,1,0:T(8,128)} %stack.20), calls=%async_computation.4 | async-start | bytes 524288 | tf_op jit(solution)/shard_map/all_to_all | solution.py:139
  333.8 12.8 %collective-permute-start.23 = (f32[1,12,4,128]{3,2,1,0:T(4,128)S(1)}, f32[1,12,4,128]{3,2,1,0:T(4,128)S(1)}, u32[]{:S(2)}, u32[]{:S(2)}) collective-permute-start(f32[1,12,4,128]{3,2,1,0:T(4,128)S(1)} %get-tuple-element.27), channel_id=1, source_target_pairs={{16,0},{32,16},{48,32},{64,48},{80,64},{96,80},{112,96},{128,112},... | collective-permute-start | bytes 73736 | tf_op jit(solution)/shard_map/ppermute | solution.py:22
  335.1 12.3 %collective-permute-start.22 = (f32[1,12,4,128]{3,2,1,0:T(4,128)S(1)}, f32[1,12,4,128]{3,2,1,0:T(4,128)S(1)}, u32[]{:S(2)}, u32[]{:S(2)}) collective-permute-start(f32[1,12,4,128]{3,2,1,0:T(4,128)S(1)} %get-tuple-element.26), channel_id=1, source_target_pairs={{0,16},{16,32},{32,48},{48,64},{64,80},{80,96},{96,112},{112,128},... | collective-permute-start | bytes 73736 | tf_op jit(solution)/shard_map/ppermute | solution.py:19
  352.6 50.8 %copy-start.24 = (s32[256]{0:T(256)S(1)}, s32[256]{0:T(256)}, u32[]{:S(2)}) copy-start(s32[256]{0:T(256)} %param.29) | copy-start | bytes 3076
  352.6 50.8 %copy-start.25 = (s32[256]{0:T(256)S(1)}, s32[256]{0:T(256)}, u32[]{:S(2)}) copy-start(s32[256]{0:T(256)} %param.28) | copy-start | bytes 3076
  352.6 50.8 %copy-start.26 = (s32[256]{0:T(256)S(1)}, s32[256]{0:T(256)}, u32[]{:S(2)}) copy-start(s32[256]{0:T(256)} %param.27) | copy-start | bytes 3076
  382.7 103.6 %collective-permute-start.19 = (f32[4,64,4,128]{3,2,1,0:T(4,128)}, f32[4,64,4,128]{3,2,1,0:T(4,128)}, u32[]{:S(2)}, u32[]{:S(2)}) collective-permute-start(f32[4,64,4,128]{3,2,1,0:T(4,128)} %get-tuple-element.16), channel_id=1, source_target_pairs={{16,0},{32,16},{48,32},{64,48},{80,64},{96,80},{112,96},{128,112},... | collective-permute-start | bytes 1572872 | tf_op jit(solution)/shard_map/ppermute | solution.py:22
  384.0 102.4 %collective-permute-start.18 = (f32[4,64,4,128]{3,2,1,0:T(4,128)}, f32[4,64,4,128]{3,2,1,0:T(4,128)}, u32[]{:S(2)}, u32[]{:S(2)}) collective-permute-start(f32[4,64,4,128]{3,2,1,0:T(4,128)} %get-tuple-element.15), channel_id=1, source_target_pairs={{0,16},{16,32},{32,48},{48,64},{64,80},{80,96},{96,112},{112,128},... | collective-permute-start | bytes 1572872 | tf_op jit(solution)/shard_map/ppermute | solution.py:19
  394.7 96.8 %all-to-all-start.5 = ((f32[16,4,8,128]{3,2,1,0:T(8,128)}), f32[16,4,8,128]{3,2,1,0:T(8,128)}, u32[]{:S(2)}, u32[]{:S(2)}) async-start(f32[16,4,8,128]{3,2,1,0:T(8,128)} %stack.21), calls=%async_computation.5 | async-start | bytes 524288 | tf_op jit(solution)/shard_map/all_to_all | solution.py:139
  430.7 27.9 %copy-start.3 = (f32[4,64,8,128]{3,2,1,0:T(8,128)S(1)}, f32[4,64,8,128]{3,2,1,0:T(8,128)}, u32[]{:S(2)}) copy-start(f32[4,64,8,128]{3,2,1,0:T(8,128)} %copy-done.2) | copy-start | bytes 3145732
  520.5 28.2 %copy-start.11 = (f32[256,4]{1,0:T(8,128)S(1)}, f32[256,4]{1,0:T(8,128)}, u32[]{:S(2)}) copy-start(f32[256,4]{1,0:T(8,128)} %gather_fusion.1) | copy-start | bytes 12292
  520.5 28.2 %copy-start.12 = (f32[256,4]{1,0:T(8,128)S(1)}, f32[256,4]{1,0:T(8,128)}, u32[]{:S(2)}) copy-start(f32[256,4]{1,0:T(8,128)} %gather_fusion.2) | copy-start | bytes 12292
  520.5 200.4 %copy-start.1 = (bf16[4,32,32,128]{3,2,1,0:T(8,128)(2,1)S(1)}, bf16[4,32,32,128]{3,2,1,0:T(8,128)(2,1)}, u32[]{:S(2)}) copy-start(bf16[4,32,32,128]{3,2,1,0:T(8,128)(2,1)} %param.22) | copy-start | bytes 3145732
  (9 other events, 92.9 us)
